TPU v7x, 32 devices: a whole 2x2x4 slice. The times are simulated.
32 devices in a mesh: frame: 8 (over z, y), head: 4 (over x, core).
Axes of the slice: x: 2, y: 2, z: 4, core: 2. Of those that a mesh axis runs over, the one named last changes fastest.
Arguments:
- queries: bfloat16 [4096, 1024], P(None, 'head'), may hold values from -8 to 8
- keys: bfloat16 [8192, 1024], P(('frame', 'head')), may hold values from -8 to 8
- values: bfloat16 [8192, 1024], P(('frame', 'head')), may hold values from -6 to 6
Outputs:
- attended: bfloat16 [4096, 1024], P('frame', 'head')
All inputs are finite; a program needn't handle non-finite values.
Results may differ from a plain program's by a relative error of at most 0.0049.
Values may be sent and summed in bfloat16 or wider, within the bound.
A program may use at most 64 MiB of HBM per device.

v0:
```python
import jax
import jax.numpy as jnp
from jax import lax
from jax.sharding import PartitionSpec as P

HEAD_DIM = 64


def widen(factor):
    return jnp.repeat(factor, HEAD_DIM, axis=1)


def local(queries, keys, values):
    key_rows, value_rows = (
        lax.all_to_all(keys, "head", split_axis=1, concat_axis=0, tiled=True),
        lax.all_to_all(values, "head", split_axis=1, concat_axis=0, tiled=True),
    )
    rows = key_rows.shape[0]
    width = key_rows.shape[1]
    heads_here = width // HEAD_DIM
    count = queries.shape[0]
    scale = HEAD_DIM ** (-0.5)
    block = min(256, rows)
    turns = rows // block
    key_blocks = key_rows.reshape(turns, block, heads_here, HEAD_DIM)
    value_blocks = value_rows.reshape(turns, block, heads_here, HEAD_DIM)
    query_heads = queries.reshape(count, heads_here, HEAD_DIM)

    def block_scores(key_block):
        return (
            jnp.einsum("qhd,khd->qhk", query_heads, key_block, preferred_element_type=jnp.float32)
            * scale
        )

    def find_top(best, key_block):
        return (jnp.maximum(best, jnp.max(block_scores(key_block), axis=2)), None)

    local_top, unused = lax.scan(
        find_top, jnp.full((count, heads_here), -1e30, jnp.float32), key_blocks
    )
    top = lax.pmax(local_top, "frame")

    def visit(carry, pair):
        total, gathered = carry
        key_block, value_block = pair
        weights = jnp.exp(block_scores(key_block) - top[:, :, None])
        total = total + jnp.sum(weights, axis=2)
        gathered = gathered + jnp.einsum(
            "qhk,khd->qhd",
            weights.astype(jnp.bfloat16),
            value_block,
            preferred_element_type=jnp.float32,
        )
        return ((total, gathered), None)

    start_state = (
        jnp.zeros((count, heads_here), jnp.float32),
        jnp.zeros((count, heads_here, HEAD_DIM), jnp.float32),
    )
    (total, gathered), unused = lax.scan(visit, start_state, (key_blocks, value_blocks))
    gathered = gathered.reshape(count, width)
    summed, mixed = (
        lax.psum_scatter(total, "frame", scatter_dimension=0, tiled=True),
        lax.psum_scatter(gathered, "frame", scatter_dimension=0, tiled=True),
    )
    return (mixed / widen(summed)).astype(jnp.bfloat16)


def solution(mesh):
    placed = (P(None, "head"), P(("frame", "head"), None), P(("frame", "head"), None))
    return jax.shard_map(
        local, mesh=mesh, in_specs=placed, out_specs=P("frame", "head"), check_vma=False
    )
```

profile of v0, /device:TPU:0, one launch (start us, length us, event | category | flops | bytes accessed | tf_op | source)
XLA Modules:
  0.0 327.8 jit_solution(15818109499562793793)
XLA Ops:
  6.5 2.0 copy.21
  8.6 4.2 %all-to-all-start = ((bf16[256,4,256]{0,2,1:T(8,128)(2,1)}), bf16[256,4,256]{0,2,1:T(8,128)(2,1)S(1)}, u32[]{:S(2)}, u32[]{:S(2)}) async-start(bf16[256,4,256]{0,2,1:T(8,128)(2,1)} %bitcast), calls=%async_computation | async-start | bytes 1048576 | tf_op jit(solution)/shard_map/all_to_all | solution.py:15
  12.8 2.1 copy.22
  14.8 4.1 %copy.17 = bf16[4096,256]{0,1:T(8,128)(2,1)} copy(bf16[4096,256]{1,0:T(8,128)(2,1)} %param.7) | data formatting | bytes 4194304 | tf_op args[0]
  18.9 2.7 all-to-all-done
  21.6 3.5 %all-to-all-start.1 = ((bf16[256,4,256]{0,2,1:T(8,128)(2,1)}), bf16[256,4,256]{0,2,1:T(8,128)(2,1)S(1)}, u32[]{:S(2)}, u32[]{:S(2)}) async-start(bf16[256,4,256]{0,2,1:T(8,128)(2,1)} %bitcast.5), calls=%async_computation.1 | async-start | bytes 1048576 | tf_op jit(solution)/shard_map/all_to_all | solution.py:16
  25.1 0.0 all-reduce.2.cloned.1.call-start
  25.1 16.2 %while.24 = (s32[]{:T(128)}, f32[4096,4]{0,1:T(4,128)S(1)}, bf16[4,256,4,64]{1,3,2,0:T(8,128)(2,1)S(1)}, bf16[4096,4,64]{0,2,1:T(8,128)(2,1)}, s32[]{:T(128)}, /*index=5*/s32[]{:T(128)}) while((s32[]{:T(128)}, f32[4096,4]{0,1:T(4,128)S(1)}, bf16[4,256,4,64]{1,3,2,0:T(8,128)(2,1)S(1)}, bf16[4096,4,64]{0,2,1:T(8,128)(2,1)}, ...), condition=%wide.region_2.3_spmd.clone, body=%wide.region_0.2_spmd.clone.sunk | while | flops 545275904 | bytes 2490459 | solution.py:38
  25.2 4.0 %multiply_reduce_fusion.2 = f32[4,4096]{1,0:T(4,128)S(1)} fusion(bf16[4096,4,64]{0,2,1:T(8,128)(2,1)} %get-tuple-element.218, bf16[4,256,4,64]{1,3,2,0:T(8,128)(2,1)S(1)} %get-tuple-element.217, s32[]{:T(128)S(6)} %copy.27), kind=kOutput, calls=%fused_computation.clone.1 | convolution fusion | flops 545243136 | bytes 2293764 | tf_op jit(solution)/shard_map/while/body/eval_jaxpr/qhd,khd->qhk/dot_general | solution.py:31
  29.2 4.0 %multiply_reduce_fusion.2 = f32[4,4096]{1,0:T(4,128)S(1)} fusion(bf16[4096,4,64]{0,2,1:T(8,128)(2,1)} %get-tuple-element.218, bf16[4,256,4,64]{1,3,2,0:T(8,128)(2,1)S(1)} %get-tuple-element.217, s32[]{:T(128)S(6)} %copy.27), kind=kOutput, calls=%fused_computation.clone.1 | convolution fusion | flops 545243136 | bytes 2293764 | tf_op jit(solution)/shard_map/while/body/eval_jaxpr/qhd,khd->qhk/dot_general | solution.py:31
  33.3 4.0 %multiply_reduce_fusion.2 = f32[4,4096]{1,0:T(4,128)S(1)} fusion(bf16[4096,4,64]{0,2,1:T(8,128)(2,1)} %get-tuple-element.218, bf16[4,256,4,64]{1,3,2,0:T(8,128)(2,1)S(1)} %get-tuple-element.217, s32[]{:T(128)S(6)} %copy.27), kind=kOutput, calls=%fused_computation.clone.1 | convolution fusion | flops 545243136 | bytes 2293764 | tf_op jit(solution)/shard_map/while/body/eval_jaxpr/qhd,khd->qhk/dot_general | solution.py:31
  37.3 4.0 %multiply_reduce_fusion.2 = f32[4,4096]{1,0:T(4,128)S(1)} fusion(bf16[4096,4,64]{0,2,1:T(8,128)(2,1)} %get-tuple-element.218, bf16[4,256,4,64]{1,3,2,0:T(8,128)(2,1)S(1)} %get-tuple-element.217, s32[]{:T(128)S(6)} %copy.27), kind=kOutput, calls=%fused_computation.clone.1 | convolution fusion | flops 545243136 | bytes 2293764 | tf_op jit(solution)/shard_map/while/body/eval_jaxpr/qhd,khd->qhk/dot_general | solution.py:31
  41.4 0.0 copy-start.3
  41.4 0.6 copy-done.3
  42.0 0.0 all-reduce.2.cloned.1.call-update
  42.0 0.0 reduce-scatter.7.cloned.1.call-start
  42.1 0.0 all-to-all-done.1
  42.1 71.0 %all-reduce.2.cloned.1.call-done = f32[4096,4]{0,1:T(4,128)} async-done(((f32[4096,4]{0,1:T(4,128)}), f32[4096,4]{0,1:T(4,128)}) %all-reduce.2.cloned.1.call-update) | async-done | bytes 65552 | tf_op jit(solution)/shard_map/pmax | solution.py:41
  113.1 45.1 %while.25 = (s32[]{:T(128)}, f32[4096,4]{0,1:T(4,128)S(1)}, f32[4096,4,64]{0,2,1:T(8,128)}, bf16[4,256,4,64]{1,3,2,0:T(8,128)(2,1)S(1)}, bf16[4096,4,64]{0,2,1:T...) while((s32[]{:T(128)}, f32[4096,4]{0,1:T(4,128)S(1)}, ...), condition=%wide.region_6.7_spmd.clone, body=%wide.region_4.6_spmd.clone.sunk | while | flops 1101021184 | bytes 78512328 | solution.py:60
  113.1 0.0 copy-start
  113.1 0.0 copy-start.2
  113.1 5.4 %fusion.39 = (f32[4096,4]{0,1:T(4,128)S(1)}, f32[4,256,4096]{2,1,0:T(8,128)S(1)}) fusion(f32[4096,4]{0,1:T(4,128)} %get-tuple-element.244, bf16[4096,4,64]{0,2,1:T(8,128)(2,1)} %get-tuple-element.243, bf16[4,256,4,64]{1,3,2,0:T(8,128)(2,1)S(1)} %get-tuple-element.242, s32[]{:T(128)S(6)} %copy.35), kind=kOutput, calls=%fused_computation.8.clone.1 | convolution fusion | flops 549437440 | bytes 19136516 | tf_op jit(solution)/shard_map/while/body/eval_jaxpr/qhd,khd->qhk/dot_general | solution.py:31
  118.5 0.1 select_add_fusion.2
  118.6 0.0 copy-done
  118.6 0.0 copy-done.2
  118.6 3.8 %fusion.40 = f32[4096,4,64]{0,2,1:T(8,128)S(1)} fusion(f32[4,256,4096]{2,1,0:T(8,128)S(1)} %get-tuple-element.202, f32[4096,4]{0,1:T(4,128)S(1)} %copy-done.2, f32[4096,4,64]{0,2,1:T(8,128)S(1)} %copy-done, pred[]{:T(512)S(6)} %compare.7, bf16[4,256,4,64]{1,3,2,0:T(8,128)(2,1)S(1)} %get-tuple-element.245, s32[]{:T(128)S(6)} %copy.35), kind=kOutput, calls=%fused_computation.13.clone.1 | convolution fusion | flops 551550976 | bytes 25362436 | tf_op jit(solution)/shard_map/while/body/eval_jaxpr/qhk,khd->qhd/dot_general | solution.py:48
  122.4 0.0 copy-start.1
  122.4 1.9 copy-done.1
  124.4 0.0 copy-start
  124.4 0.0 copy-start.2
  124.4 5.4 %fusion.39 = (f32[4096,4]{0,1:T(4,128)S(1)}, f32[4,256,4096]{2,1,0:T(8,128)S(1)}) fusion(f32[4096,4]{0,1:T(4,128)} %get-tuple-element.244, bf16[4096,4,64]{0,2,1:T(8,128)(2,1)} %get-tuple-element.243, bf16[4,256,4,64]{1,3,2,0:T(8,128)(2,1)S(1)} %get-tuple-element.242, s32[]{:T(128)S(6)} %copy.35), kind=kOutput, calls=%fused_computation.8.clone.1 | convolution fusion | flops 549437440 | bytes 19136516 | tf_op jit(solution)/shard_map/while/body/eval_jaxpr/qhd,khd->qhk/dot_general | solution.py:31
  129.8 0.1 select_add_fusion.2
  129.9 0.0 copy-done
  129.9 0.0 copy-done.2
  129.9 3.8 %fusion.40 = f32[4096,4,64]{0,2,1:T(8,128)S(1)} fusion(f32[4,256,4096]{2,1,0:T(8,128)S(1)} %get-tuple-element.202, f32[4096,4]{0,1:T(4,128)S(1)} %copy-done.2, f32[4096,4,64]{0,2,1:T(8,128)S(1)} %copy-done, pred[]{:T(512)S(6)} %compare.7, bf16[4,256,4,64]{1,3,2,0:T(8,128)(2,1)S(1)} %get-tuple-element.245, s32[]{:T(128)S(6)} %copy.35), kind=kOutput, calls=%fused_computation.13.clone.1 | convolution fusion | flops 551550976 | bytes 25362436 | tf_op jit(solution)/shard_map/while/body/eval_jaxpr/qhk,khd->qhd/dot_general | solution.py:48
  133.7 0.0 copy-start.1
  133.7 1.9 copy-done.1
  135.6 0.0 copy-start
  135.6 0.0 copy-start.2
  135.6 5.4 %fusion.39 = (f32[4096,4]{0,1:T(4,128)S(1)}, f32[4,256,4096]{2,1,0:T(8,128)S(1)}) fusion(f32[4096,4]{0,1:T(4,128)} %get-tuple-element.244, bf16[4096,4,64]{0,2,1:T(8,128)(2,1)} %get-tuple-element.243, bf16[4,256,4,64]{1,3,2,0:T(8,128)(2,1)S(1)} %get-tuple-element.242, s32[]{:T(128)S(6)} %copy.35), kind=kOutput, calls=%fused_computation.8.clone.1 | convolution fusion | flops 549437440 | bytes 19136516 | tf_op jit(solution)/shard_map/while/body/eval_jaxpr/qhd,khd->qhk/dot_general | solution.py:31
  141.1 0.1 select_add_fusion.2
  141.2 0.0 copy-done
  141.2 0.0 copy-done.2
  141.2 3.8 %fusion.40 = f32[4096,4,64]{0,2,1:T(8,128)S(1)} fusion(f32[4,256,4096]{2,1,0:T(8,128)S(1)} %get-tuple-element.202, f32[4096,4]{0,1:T(4,128)S(1)} %copy-done.2, f32[4096,4,64]{0,2,1:T(8,128)S(1)} %copy-done, pred[]{:T(512)S(6)} %compare.7, bf16[4,256,4,64]{1,3,2,0:T(8,128)(2,1)S(1)} %get-tuple-element.245, s32[]{:T(128)S(6)} %copy.35), kind=kOutput, calls=%fused_computation.13.clone.1 | convolution fusion | flops 551550976 | bytes 25362436 | tf_op jit(solution)/shard_map/while/body/eval_jaxpr/qhk,khd->qhd/dot_general | solution.py:48
  145.0 0.0 copy-start.1
  145.0 1.9 copy-done.1
  146.9 0.0 copy-start
  146.9 0.0 copy-start.2
  146.9 5.4 %fusion.39 = (f32[4096,4]{0,1:T(4,128)S(1)}, f32[4,256,4096]{2,1,0:T(8,128)S(1)}) fusion(f32[4096,4]{0,1:T(4,128)} %get-tuple-element.244, bf16[4096,4,64]{0,2,1:T(8,128)(2,1)} %get-tuple-element.243, bf16[4,256,4,64]{1,3,2,0:T(8,128)(2,1)S(1)} %get-tuple-element.242, s32[]{:T(128)S(6)} %copy.35), kind=kOutput, calls=%fused_computation.8.clone.1 | convolution fusion | flops 549437440 | bytes 19136516 | tf_op jit(solution)/shard_map/while/body/eval_jaxpr/qhd,khd->qhk/dot_general | solution.py:31
  152.4 0.1 select_add_fusion.2
  152.4 0.0 copy-done
  152.4 0.0 copy-done.2
  152.4 3.8 %fusion.40 = f32[4096,4,64]{0,2,1:T(8,128)S(1)} fusion(f32[4,256,4096]{2,1,0:T(8,128)S(1)} %get-tuple-element.202, f32[4096,4]{0,1:T(4,128)S(1)} %copy-done.2, f32[4096,4,64]{0,2,1:T(8,128)S(1)} %copy-done, pred[]{:T(512)S(6)} %compare.7, bf16[4,256,4,64]{1,3,2,0:T(8,128)(2,1)S(1)} %get-tuple-element.245, s32[]{:T(128)S(6)} %copy.35), kind=kOutput, calls=%fused_computation.13.clone.1 | convolution fusion | flops 551550976 | bytes 25362436 | tf_op jit(solution)/shard_map/while/body/eval_jaxpr/qhk,khd->qhd/dot_general | solution.py:48
  156.3 0.0 copy-start.1
  156.3 1.9 copy-done.1
  158.2 2.0 copy.23
  160.2 0.0 reduce-scatter.7.cloned.1.call-update
  160.2 0.0 reduce-scatter.5.cloned.1.call-start
  160.2 0.7 reduce-scatter.5.cloned.1.call-update
  160.9 67.1 %reduce-scatter.7.cloned.1.call-done = f32[512,4]{1,0:T(8,128)} async-done(((f32[4096,4]{1,0:T(8,128)}), f32[512,4]{1,0:T(8,128)}) %reduce-scatter.7.cloned.1.call-update) | async-done | bytes 8208
  228.0 1.1 copy.24
  229.0 90.3 %reduce-scatter.5.cloned.1.call-done = f32[512,256]{0,1:T(8,128)} async-done(((f32[4096,256]{0,1:T(8,128)}), f32[512,256]{0,1:T(8,128)}) %reduce-scatter.5.cloned.1.call-update) | async-done | bytes 524304 | tf_op jit(solution)/shard_map/reduce_scatter | solution.py:64
  319.4 1.1 fusion.24
  320.4 0.8 copy.19
  (7 shorter events, 0.1 us)
Async XLA Ops:
  8.6 13.1 %all-to-all-start = ((bf16[256,4,256]{0,2,1:T(8,128)(2,1)}), bf16[256,4,256]{0,2,1:T(8,128)(2,1)S(1)}, u32[]{:S(2)}, u32[]{:S(2)}) async-start(bf16[256,4,256]{0,2,1:T(8,128)(2,1)} %bitcast), calls=%async_computation | async-start | bytes 1048576 | tf_op jit(solution)/shard_map/all_to_all | solution.py:15
  21.6 20.5 %all-to-all-start.1 = ((bf16[256,4,256]{0,2,1:T(8,128)(2,1)}), bf16[256,4,256]{0,2,1:T(8,128)(2,1)S(1)}, u32[]{:S(2)}, u32[]{:S(2)}) async-start(bf16[256,4,256]{0,2,1:T(8,128)(2,1)} %bitcast.5), calls=%async_computation.1 | async-start | bytes 1048576 | tf_op jit(solution)/shard_map/all_to_all | solution.py:16
  25.1 88.0 %all-reduce.2.cloned.1.call-start = ((), (), s32[]{:S(2)}) async-start(), calls=%async_computation.4 | async-start | bytes 131072 | tf_op jit(solution)/shard_map/pmax | solution.py:41
  41.4 0.6 copy-start.3
  42.0 186.0 %reduce-scatter.7.cloned.1.call-start = ((), (), s32[]{:S(2)}) async-start(), calls=%async_computation.6 | async-start | bytes 2359296
  113.1 5.5 %copy-start = (f32[4096,4,64]{0,2,1:T(8,128)S(1)}, f32[4096,4,64]{0,2,1:T(8,128)}, u32[]{:S(2)}) copy-start(f32[4096,4,64]{0,2,1:T(8,128)} %get-tuple-element.232) | copy-start | bytes 12582916 | tf_op jit(solution)/shard_map/while
  113.1 5.5 %copy-start.2 = (f32[4096,4]{0,1:T(4,128)S(1)}, f32[4096,4]{0,1:T(4,128)}, u32[]{:S(2)}) copy-start(f32[4096,4]{0,1:T(4,128)} %get-tuple-element.244) | copy-start | bytes 196612 | tf_op jit(solution)/shard_map/while
  122.4 1.9 copy-start.1
  124.4 5.5 %copy-start = (f32[4096,4,64]{0,2,1:T(8,128)S(1)}, f32[4096,4,64]{0,2,1:T(8,128)}, u32[]{:S(2)}) copy-start(f32[4096,4,64]{0,2,1:T(8,128)} %get-tuple-element.232) | copy-start | bytes 12582916 | tf_op jit(solution)/shard_map/while
  124.4 5.5 %copy-start.2 = (f32[4096,4]{0,1:T(4,128)S(1)}, f32[4096,4]{0,1:T(4,128)}, u32[]{:S(2)}) copy-start(f32[4096,4]{0,1:T(4,128)} %get-tuple-element.244) | copy-start | bytes 196612 | tf_op jit(solution)/shard_map/while
  133.7 1.9 copy-start.1
  135.6 5.5 %copy-start = (f32[4096,4,64]{0,2,1:T(8,128)S(1)}, f32[4096,4,64]{0,2,1:T(8,128)}, u32[]{:S(2)}) copy-start(f32[4096,4,64]{0,2,1:T(8,128)} %get-tuple-element.232) | copy-start | bytes 12582916 | tf_op jit(solution)/shard_map/while
  135.6 5.5 %copy-start.2 = (f32[4096,4]{0,1:T(4,128)S(1)}, f32[4096,4]{0,1:T(4,128)}, u32[]{:S(2)}) copy-start(f32[4096,4]{0,1:T(4,128)} %get-tuple-element.244) | copy-start | bytes 196612 | tf_op jit(solution)/shard_map/while
  145.0 1.9 copy-start.1
  146.9 5.5 %copy-start = (f32[4096,4,64]{0,2,1:T(8,128)S(1)}, f32[4096,4,64]{0,2,1:T(8,128)}, u32[]{:S(2)}) copy-start(f32[4096,4,64]{0,2,1:T(8,128)} %get-tuple-element.232) | copy-start | bytes 12582916 | tf_op jit(solution)/shard_map/while
  146.9 5.5 %copy-start.2 = (f32[4096,4]{0,1:T(4,128)S(1)}, f32[4096,4]{0,1:T(4,128)}, u32[]{:S(2)}) copy-start(f32[4096,4]{0,1:T(4,128)} %get-tuple-element.244) | copy-start | bytes 196612 | tf_op jit(solution)/shard_map/while
  156.3 1.9 copy-start.1
  160.2 159.2 %reduce-scatter.5.cloned.1.call-start = ((), (), s32[]{:S(2)}) async-start(), calls=%async_computation.5 | async-start | bytes 4718592 | tf_op jit(solution)/shard_map/reduce_scatter | solution.py:64
Sparse Core Ops, SparseCore 0:
  42.1 70.9 all-reduce.1
  160.3 67.6 reduce-scatter.6
  232.1 87.2 reduce-scatter.4
where the time goes:
time: 328 us
  waiting for transfers between devices  232 us (71%)
  matrix products  52.9 us (16%)
  local copies, waits for them, and re-layouts  20.4 us (6%)
  between operations  13.2 us (4%)
  starting transfers between devices  7.8 us (2%)
    reduce_scatter x1, waiting for transfers between devices, local(): lax.psum_scatter(gathered, 'frame', scatter_dimension=0, tiled=True)  90.3 us
    pmax x1, waiting for transfers between devices, local(): top = lax.pmax(local_top, 'frame')  71 us
    unnamed x4, waiting for transfers between devices  67.8 us
    dot_general x8, matrix products, block_scores(): jnp.einsum('qhd,khd->qhk', query_heads, key_block, preferred_element_type...  37.7 us
    dot_general x4, matrix products, visit(): jnp.einsum('qhk,khd->qhd', weights.astype(jnp.bfloat16), value_block, pre...  15.2 us
    while x24, local copies, waits for them, and re-layouts  7.73 us
    unnamed x5, local copies, waits for them, and re-layouts  7.72 us
  transfers between devices with their start and end apart: 5, of which 4 were waited for; matrix products, arithmetic and copies ran while one was open for 7% of the time, Pallas kernels for 0%

commit v1 on v0

v1 whole, which is shorter than its diff:
```python
import functools

import jax
import jax.numpy as jnp
from jax import lax
from jax.experimental import pallas as pl
from jax.experimental.pallas import tpu as pltpu
from jax.sharding import PartitionSpec as P

HEAD_DIM = 64
ONES = 16
LSE_ROWS = 32
MESH = pl.DeviceIdType.MESH


def bit(value, place):
    return (value // (1 << place)) % 2


def prepare(key_block, value_block, masked_ref, turned_ref, start, heads):
    rows, width = key_block.shape
    column = lax.broadcasted_iota(jnp.int32, (rows, width), 1)
    scaled = key_block.astype(jnp.float32) * (HEAD_DIM ** -0.5)
    turned = value_block.astype(jnp.float32).T.astype(jnp.bfloat16)
    for h in range(heads):
        own = (column >= h * HEAD_DIM) & (column < (h + 1) * HEAD_DIM)
        masked_ref[h, pl.ds(start, rows), :] = jnp.where(own, scaled, 0.0).astype(jnp.bfloat16)
        turned_ref[h, 0:HEAD_DIM, pl.ds(start, rows)] = turned[h * HEAD_DIM : (h + 1) * HEAD_DIM]
        turned_ref[h, HEAD_DIM : HEAD_DIM + ONES, pl.ds(start, rows)] = jnp.ones(
            (ONES, rows), jnp.bfloat16
        )


def kernel(
    frames, groups, stages, tile, per_block, heads,
    q_ref, k_ref, v_ref, out_ref,
    k_got, v_got, masked_own, turned_own, masked_rest, turned_rest,
    q_turned, early, early_top, mixed, lse, outbox, inbox,
    k_send, k_recv, v_send, v_recv, part_send, part_recv,
):
    frame = lax.axis_index("frame")
    group = lax.axis_index("head")
    rows = k_ref.shape[0]
    width = q_ref.shape[1]
    wide = HEAD_DIM + ONES
    tiles = frames * per_block

    def partner(stage):
        return frame + (1 << stage) * (1 - 2 * bit(frame, stage))

    barrier = pltpu.get_barrier_semaphore()
    for d in range(1, groups):
        pl.semaphore_signal(
            barrier, inc=1, device_id=(frame, lax.rem(group + d, groups)), device_id_type=MESH
        )
    for s in range(stages):
        pl.semaphore_signal(barrier, inc=1, device_id=(partner(s), group), device_id_type=MESH)
    pl.semaphore_wait(barrier, groups - 1 + stages)

    def exchange(d):
        to = lax.rem(group + d, groups)
        columns = pl.ds(pl.multiple_of(to * width, width), width)
        return [
            pltpu.make_async_remote_copy(
                src_ref=ref.at[:, columns],
                dst_ref=got.at[d - 1],
                send_sem=send.at[d - 1],
                recv_sem=recv.at[d - 1],
                device_id=(frame, to),
                device_id_type=MESH,
            )
            for ref, got, send, recv in ((k_ref, k_got, k_send, k_recv), (v_ref, v_got, v_send, v_recv))
        ]

    for d in range(1, groups):
        for copy in exchange(d):
            copy.start()

    mine = pl.ds(pl.multiple_of(group * width, width), width)
    prepare(k_ref[:, mine], v_ref[:, mine], masked_own, turned_own, 0, heads)

    def attend_own(t, carry):
        q = q_ref[pl.ds(pl.multiple_of(t * tile, tile), tile), :].T
        q_turned[t] = q
        tops = []
        for h in range(heads):
            scores = jnp.dot(masked_own[h], q, preferred_element_type=jnp.float32)
            top = jnp.max(scores, axis=0, keepdims=True)
            weights = jnp.exp(scores - top).astype(jnp.bfloat16)
            early[t, h * wide : (h + 1) * wide] = jnp.dot(
                turned_own[h], weights, preferred_element_type=jnp.float32
            )
            early_top[t, h : h + 1, :] = top
        return carry

    lax.fori_loop(0, tiles, attend_own, 0)

    for d in range(1, groups):
        for copy in exchange(d):
            copy.wait_recv()
        prepare(k_got[d - 1], v_got[d - 1], masked_rest, turned_rest, (d - 1) * rows, heads)

    def part_copy(stage, slot):
        return pltpu.make_async_remote_copy(
            src_ref=outbox.at[slot],
            dst_ref=inbox.at[slot],
            send_sem=part_send.at[slot],
            recv_sem=part_recv.at[slot],
            device_id=(partner(stage), group),
            device_id_type=MESH,
        )

    def slot_of(stage, rel, j):
        first = frames - (frames >> stage)
        return (first + rel // (1 << (stage + 1))) * per_block + j

    lse[...] = jnp.zeros_like(lse)

    def attend_rest(i, carry):
        order = i // per_block
        j = i % per_block
        rel = 0
        block = 0
        for s in range(stages):
            r = 1 - bit(order, stages - 1 - s)
            rel = rel + (1 << s) * r
            block = block + (1 << s) * ((bit(frame, s) + r) % 2)
        t = block * per_block + j
        q = q_turned[t]
        for h in range(heads):
            scores = jnp.dot(masked_rest[h], q, preferred_element_type=jnp.float32)
            before = early_top[t, h : h + 1, :]
            top = jnp.maximum(jnp.max(scores, axis=0, keepdims=True), before)
            weights = jnp.exp(scores - top).astype(jnp.bfloat16)
            both = jnp.dot(turned_rest[h], weights, preferred_element_type=jnp.float32)
            both = both + early[t, h * wide : (h + 1) * wide] * jnp.exp(before - top)
            total = both[HEAD_DIM : HEAD_DIM + 1]
            mixed[h * HEAD_DIM : (h + 1) * HEAD_DIM, :] = both[:HEAD_DIM] * (1.0 / total)
            lse[h : h + 1, :] = top + jnp.log(total)

        for s in range(stages):
            @pl.when(rel % (1 << (s + 1)) == 0)
            def _():
                slot = slot_of(s, rel, j)
                part_copy(s, slot).wait_recv()
                packed = inbox[slot, width:, :].astype(jnp.float32)
                other = packed[0:8] + packed[8:16] + packed[16:24]
                here = lse[...]
                top = jnp.maximum(here, other)
                a = jnp.exp(here - top)
                b = jnp.exp(other - top)
                total = a + b
                a = a / total
                b = b / total
                lse[...] = top + jnp.log(total)
                for h in range(heads):
                    part = slice(h * HEAD_DIM, (h + 1) * HEAD_DIM)
                    mixed[part, :] = (
                        mixed[part, :] * a[h : h + 1]
                        + inbox[slot, part, :].astype(jnp.float32) * b[h : h + 1]
                    )

        for s in range(stages):
            @pl.when(rel % (1 << (s + 1)) == (1 << s))
            def _():
                slot = slot_of(s, rel, j)
                outbox[slot, :width, :] = mixed[...].astype(jnp.bfloat16)
                rest = lse[...]
                pieces = []
                for _ in range(3):
                    piece = rest.astype(jnp.bfloat16).astype(jnp.float32)
                    pieces.append(piece)
                    rest = rest - piece
                pieces.append(jnp.zeros_like(rest))
                outbox[slot, width:, :] = jnp.concatenate(pieces, axis=0).astype(jnp.bfloat16)
                part_copy(s, slot).start()

        @pl.when(rel == 0)
        def _():
            out_ref[pl.ds(pl.multiple_of(j * tile, tile), tile), :] = mixed[...].T.astype(
                out_ref.dtype
            )

        return carry

    lax.fori_loop(0, tiles, attend_rest, 0)

    for s in range(stages):
        first = (frames - (frames >> s)) * per_block
        count = (frames >> (s + 1)) * per_block

        def drain(n, carry):
            part_copy(s, first + n).wait_send()
            return carry

        lax.fori_loop(0, count, drain, 0)
    for d in range(1, groups):
        for copy in exchange(d):
            copy.wait_send()


def local(frames, groups, queries, keys, values):
    count, width = queries.shape
    rows = keys.shape[0]
    heads = width // HEAD_DIM
    stages = frames.bit_length() - 1
    own = count // frames
    tile = min(256, own)
    per_block = own // tile
    tiles = count // tile
    slots = (frames - 1) * per_block
    rest = (groups - 1) * rows
    wide = HEAD_DIM + ONES
    bf16, f32 = jnp.bfloat16, jnp.float32
    dma = pltpu.SemaphoreType.DMA
    return pl.pallas_call(
        functools.partial(kernel, frames, groups, stages, tile, per_block, heads),
        out_shape=jax.ShapeDtypeStruct((own, width), bf16),
        in_specs=[pl.BlockSpec(memory_space=pltpu.VMEM)] * 3,
        out_specs=pl.BlockSpec(memory_space=pltpu.VMEM),
        scratch_shapes=[
            pltpu.VMEM((groups - 1, rows, width), bf16),
            pltpu.VMEM((groups - 1, rows, width), bf16),
            pltpu.VMEM((heads, rows, width), bf16),
            pltpu.VMEM((heads, wide, rows), bf16),
            pltpu.VMEM((heads, rest, width), bf16),
            pltpu.VMEM((heads, wide, rest), bf16),
            pltpu.VMEM((tiles, width, tile), bf16),
            pltpu.VMEM((tiles, heads * wide, tile), f32),
            pltpu.VMEM((tiles, 8, tile), f32),
            pltpu.VMEM((width, tile), f32),
            pltpu.VMEM((8, tile), f32),
            pltpu.VMEM((slots, width + LSE_ROWS, tile), bf16),
            pltpu.VMEM((slots, width + LSE_ROWS, tile), bf16),
            dma((groups - 1,)), dma((groups - 1,)), dma((groups - 1,)), dma((groups - 1,)),
            dma((slots,)), dma((slots,)),
        ],
        compiler_params=pltpu.CompilerParams(
            collective_id=0, has_side_effects=True, vmem_limit_bytes=48 * 1024 * 1024
        ),
    )(queries, keys, values)


def solution(mesh):
    placed = (P(None, "head"), P(("frame", "head"), None), P(("frame", "head"), None))
    return jax.shard_map(
        functools.partial(local, mesh.shape["frame"], mesh.shape["head"]),
        mesh=mesh, in_specs=placed, out_specs=P("frame", "head"), check_vma=False,
    )
```

time: 328 us -> 75.8 us (0.23)
  waiting for transfers between devices: 232 us -> 0 us
  Pallas kernels: 0 us -> 71.2 us
  matrix products: 52.9 us -> 0 us
  local copies, waits for them, and re-layouts: 20.4 us -> 4.38 us
  between operations: 13.2 us -> 0.01 us
  starting transfers between devices: 7.8 us -> 0 us
    reduce_scatter x1 -> x0, waiting for transfers between devices: 90.3 us -> none  [local(): lax.psum_scatter(gathered, 'frame', scatter_dimension=0, tiled=True)]
    pallas_call x0 -> x1, Pallas kernels: none -> 71.2 us  [local(): pl.pallas_call(functools.partial(kernel, frames, groups, stages, tile, pe...]
    pmax x1 -> x0, waiting for transfers between devices: 71 us -> none  [local(): top = lax.pmax(local_top, 'frame')]
    unnamed x4 -> x0, waiting for transfers between devices: 67.8 us -> none
    dot_general x12 -> x0, matrix products: 52.9 us -> none  [the longest x8 37.7 us: block_scores(): jnp.einsum('qhd,khd->qhk', query_heads, key_block, preferred_element_type...]
    while x24 -> x0, local copies, waits for them, and re-layouts: 7.73 us -> none
    all_to_all x2 -> x0, starting transfers between devices: 7.68 us -> none  [the longest x1 4.21 us: local(): lax.all_to_all(keys, 'head', split_axis=1, concat_axis=0, tiled=True)]
    all_to_all x2 -> x0, local copies, waits for them, and re-layouts: 4.08 us -> none  [the longest x1 2.05 us: local(): lax.all_to_all(values, 'head', split_axis=1, concat_axis=0, tiled=True)]
  transfers between devices with their start and end apart: 5 -> 0, of which waited for: 4 -> 0; matrix products, arithmetic and copies ran while one was open for 7% -> 0% of each run, Pallas kernels for 0% -> 0%
where the time goes in v1:
time: 75.8 us; the launch traced here: 75.5 us
  Pallas kernels  71.2 us (94%)
  local copies, waits for them, and re-layouts  4.38 us (6%)
    pallas_call x1, Pallas kernels, local(): pl.pallas_call(functools.partial(kernel, frames, groups, stages, tile, pe...  71.2 us
    unnamed x7, local copies, waits for them, and re-layouts  4.38 us

profile of v1, /device:TPU:0, one launch (start us, length us, event | category | flops | bytes accessed | tf_op | source)
XLA Modules:
  0.0 75.5 jit_solution(14486343854520357396)
XLA Ops:
  0.0 0.0 copy-start
  0.0 1.6 %copy-done = bf16[4096,256]{1,0:T(8,128)(2,1)S(1)} copy-done((bf16[4096,256]{1,0:T(8,128)(2,1)S(1)}, bf16[4096,256]{1,0:T(8,128)(2,1)}, u32[]{:S(2)}) %copy-start) | copy-done | bytes 2097176
  1.6 0.0 copy-start.1
  1.6 1.0 %copy-done.1 = bf16[256,1024]{1,0:T(8,128)(2,1)S(1)} copy-done((bf16[256,1024]{1,0:T(8,128)(2,1)S(1)}, bf16[256,1024]{1,0:T(8,128)(2,1)}, u32[]{:S(2)}) %copy-start.1) | copy-done | bytes 524312
  2.6 0.0 copy-start.2
  2.6 1.0 %copy-done.2 = bf16[256,1024]{1,0:T(8,128)(2,1)S(1)} copy-done((bf16[256,1024]{1,0:T(8,128)(2,1)S(1)}, bf16[256,1024]{1,0:T(8,128)(2,1)}, u32[]{:S(2)}) %copy-start.2) | copy-done | bytes 524312
  3.7 71.2 %shard_map.37 = bf16[512,256]{1,0:T(8,128)(2,1)S(1)} custom-call(bf16[4096,256]{1,0:T(8,128)(2,1)S(1)} %copy-done, bf16[256,1024]{1,0:T(8,128)(2,1)S(1)} %copy-done.1, bf16[256,1024]{1,0:T(8,128)(2,1)S(1)} %copy-done.2), custom_call_target="tpu_custom_call" | custom-call | tf_op jit(solution)/shard_map/pallas_call | solution.py:216
  74.8 0.7 copy.5
Async XLA Ops:
  0.0 1.6 %copy-start = (bf16[4096,256]{1,0:T(8,128)(2,1)S(1)}, bf16[4096,256]{1,0:T(8,128)(2,1)}, u32[]{:S(2)}) copy-start(bf16[4096,256]{1,0:T(8,128)(2,1)} %q_ref.1) | copy-start | bytes 6291460
  1.6 1.0 %copy-start.1 = (bf16[256,1024]{1,0:T(8,128)(2,1)S(1)}, bf16[256,1024]{1,0:T(8,128)(2,1)}, u32[]{:S(2)}) copy-start(bf16[256,1024]{1,0:T(8,128)(2,1)} %k_ref.1) | copy-start | bytes 1572868
  2.6 1.0 %copy-start.2 = (bf16[256,1024]{1,0:T(8,128)(2,1)S(1)}, bf16[256,1024]{1,0:T(8,128)(2,1)}, u32[]{:S(2)}) copy-start(bf16[256,1024]{1,0:T(8,128)(2,1)} %v_ref.1) | copy-start | bytes 1572868

commit v2 on v1

--- a/solution.py
+++ b/solution.py
@@ -10,6 +10,7 @@
 HEAD_DIM = 64
 ONES = 16
 LSE_ROWS = 32
+LOG2E = 1.4426950408889634
 MESH = pl.DeviceIdType.MESH
 
 
@@ -18,13 +19,17 @@
 
 
 def prepare(key_block, value_block, masked_ref, turned_ref, start, heads):
-    rows, width = key_block.shape
-    column = lax.broadcasted_iota(jnp.int32, (rows, width), 1)
-    scaled = key_block.astype(jnp.float32) * (HEAD_DIM ** -0.5)
+    rows = key_block.shape[0]
+    pair = 2 * HEAD_DIM
+    column = lax.broadcasted_iota(jnp.int32, (rows, pair), 1)
     turned = value_block.astype(jnp.float32).T.astype(jnp.bfloat16)
     for h in range(heads):
-        own = (column >= h * HEAD_DIM) & (column < (h + 1) * HEAD_DIM)
-        masked_ref[h, pl.ds(start, rows), :] = jnp.where(own, scaled, 0.0).astype(jnp.bfloat16)
+        first = (h // 2) * pair
+        own = (column // HEAD_DIM) == h % 2
+        kept = jnp.where(own, key_block[:, first : first + pair].astype(jnp.float32), 0.0)
+        kept = kept.astype(jnp.bfloat16)
+        masked_ref[h, pl.ds(start, rows), 0:pair] = kept
+        masked_ref[h, pl.ds(start, rows), pair : 2 * pair] = kept
         turned_ref[h, 0:HEAD_DIM, pl.ds(start, rows)] = turned[h * HEAD_DIM : (h + 1) * HEAD_DIM]
         turned_ref[h, HEAD_DIM : HEAD_DIM + ONES, pl.ds(start, rows)] = jnp.ones(
             (ONES, rows), jnp.bfloat16
@@ -33,7 +38,8 @@
 
 def kernel(
     frames, groups, stages, tile, per_block, heads,
-    q_ref, k_ref, v_ref, out_ref,
+    q_hbm, k_ref, v_ref, out_ref,
+    q_ref, k_own, v_own, score, local_sem,
     k_got, v_got, masked_own, turned_own, masked_rest, turned_rest,
     q_turned, early, early_top, mixed, lse, outbox, inbox,
     k_send, k_recv, v_send, v_recv, part_send, part_recv,
@@ -47,6 +53,15 @@
 
     def partner(stage):
         return frame + (1 << stage) * (1 - 2 * bit(frame, stage))
+
+    mine = pl.ds(pl.multiple_of(group * width, width), width)
+    fetches = [
+        pltpu.make_async_copy(k_ref.at[:, mine], k_own, local_sem.at[0]),
+        pltpu.make_async_copy(v_ref.at[:, mine], v_own, local_sem.at[1]),
+        pltpu.make_async_copy(q_hbm, q_ref, local_sem.at[2]),
+    ]
+    for fetch in fetches:
+        fetch.start()
 
     barrier = pltpu.get_barrier_semaphore()
     for d in range(1, groups):
@@ -76,24 +91,66 @@
         for copy in exchange(d):
             copy.start()
 
-    mine = pl.ds(pl.multiple_of(group * width, width), width)
-    prepare(k_ref[:, mine], v_ref[:, mine], masked_own, turned_own, 0, heads)
-
-    def attend_own(t, carry):
-        q = q_ref[pl.ds(pl.multiple_of(t * tile, tile), tile), :].T
-        q_turned[t] = q
-        tops = []
-        for h in range(heads):
-            scores = jnp.dot(masked_own[h], q, preferred_element_type=jnp.float32)
-            top = jnp.max(scores, axis=0, keepdims=True)
-            weights = jnp.exp(scores - top).astype(jnp.bfloat16)
-            early[t, h * wide : (h + 1) * wide] = jnp.dot(
-                turned_own[h], weights, preferred_element_type=jnp.float32
-            )
-            early_top[t, h : h + 1, :] = top
-        return carry
-
-    lax.fori_loop(0, tiles, attend_own, 0)
+    fetches[0].wait()
+    fetches[1].wait()
+    prepare(k_own[...], v_own[...], masked_own, turned_own, 0, heads)
+    fetches[2].wait()
+
+    def turn(t):
+        q = q_ref[pl.ds(pl.multiple_of(t * tile, tile), tile), :].astype(jnp.float32).T
+        q = q * (HEAD_DIM ** -0.5 * LOG2E)
+        high = q.astype(jnp.bfloat16)
+        low = (q - high.astype(jnp.float32)).astype(jnp.bfloat16)
+        pair = 2 * HEAD_DIM
+        for g in range(heads // 2):
+            q_turned[t, g, 0:pair, :] = high[g * pair : (g + 1) * pair]
+            q_turned[t, g, pair : 2 * pair, :] = low[g * pair : (g + 1) * pair]
+
+    def sweep(tile_of, masked, turned, floor, done):
+        depth = masked.shape[1]
+        step = min(256, depth)
+
+        def scores_of(t, h, slot, c):
+            at = slice(c * step, (c + 1) * step)
+            part = jnp.dot(masked[h, at, :], q_turned[t, h // 2], preferred_element_type=jnp.float32)
+            score[slot, at, :] = part
+            return jnp.max(part, axis=0, keepdims=True)
+
+        first = floor(tile_of(0), 0)
+        for c in range(depth // step):
+            found = scores_of(tile_of(0), 0, 0, c)
+            first = found if first is None else jnp.maximum(first, found)
+
+        def visit(i, top):
+            t = tile_of(i)
+            after = tile_of(lax.rem(i + 1, tiles))
+            if floor(t, 0) is None:
+                turn(after)
+            for h in range(heads):
+                slot = h % 2
+                where = (t, h + 1) if h + 1 < heads else (after, 0)
+                coming = floor(*where)
+                both = None
+                for c in range(depth // step):
+                    found = scores_of(*where, 1 - slot, c)
+                    coming = found if coming is None else jnp.maximum(coming, found)
+                    at = slice(c * step, (c + 1) * step)
+                    weights = jnp.exp2(score[slot, at, :] - top).astype(jnp.bfloat16)
+                    part = jnp.dot(turned[h, :, at], weights, preferred_element_type=jnp.float32)
+                    both = part if both is None else both + part
+                done(i, t, h, both, top)
+                top = coming
+            return top
+
+        return visit, first
+
+    def keep(i, t, h, both, top):
+        early[t, h * wide : (h + 1) * wide] = both
+        early_top[t, h : h + 1, :] = top
+
+    turn(0)
+    visit_own, first = sweep(lambda i: i, masked_own, turned_own, lambda t, h: None, keep)
+    lax.fori_loop(0, tiles, visit_own, first)
 
     for d in range(1, groups):
         for copy in exchange(d):
@@ -116,27 +173,32 @@
 
     lse[...] = jnp.zeros_like(lse)
 
-    def attend_rest(i, carry):
+    def place(i):
         order = i // per_block
-        j = i % per_block
         rel = 0
         block = 0
         for s in range(stages):
             r = 1 - bit(order, stages - 1 - s)
             rel = rel + (1 << s) * r
             block = block + (1 << s) * ((bit(frame, s) + r) % 2)
-        t = block * per_block + j
-        q = q_turned[t]
-        for h in range(heads):
-            scores = jnp.dot(masked_rest[h], q, preferred_element_type=jnp.float32)
-            before = early_top[t, h : h + 1, :]
-            top = jnp.maximum(jnp.max(scores, axis=0, keepdims=True), before)
-            weights = jnp.exp(scores - top).astype(jnp.bfloat16)
-            both = jnp.dot(turned_rest[h], weights, preferred_element_type=jnp.float32)
-            both = both + early[t, h * wide : (h + 1) * wide] * jnp.exp(before - top)
-            total = both[HEAD_DIM : HEAD_DIM + 1]
-            mixed[h * HEAD_DIM : (h + 1) * HEAD_DIM, :] = both[:HEAD_DIM] * (1.0 / total)
-            lse[h : h + 1, :] = top + jnp.log(total)
+        return rel, block * per_block + i % per_block
+
+    def settle(i, t, h, both, top):
+        before = early_top[t, h : h + 1, :]
+        both = both + early[t, h * wide : (h + 1) * wide] * jnp.exp2(before - top)
+        total = both[HEAD_DIM : HEAD_DIM + 1]
+        mixed[h * HEAD_DIM : (h + 1) * HEAD_DIM, :] = both[:HEAD_DIM] * (1.0 / total)
+        lse[h : h + 1, :] = top + jnp.log(total) * LOG2E
+
+    visit_rest, first = sweep(
+        lambda i: place(i)[1], masked_rest, turned_rest,
+        lambda t, h: early_top[t, h : h + 1, :], settle,
+    )
+
+    def attend_rest(i, carry):
+        j = i % per_block
+        rel, _ = place(i)
+        carry = visit_rest(i, carry)
 
         for s in range(stages):
             @pl.when(rel % (1 << (s + 1)) == 0)
@@ -147,12 +209,12 @@
                 other = packed[0:8] + packed[8:16] + packed[16:24]
                 here = lse[...]
                 top = jnp.maximum(here, other)
-                a = jnp.exp(here - top)
-                b = jnp.exp(other - top)
+                a = jnp.exp2(here - top)
+                b = jnp.exp2(other - top)
                 total = a + b
                 a = a / total
                 b = b / total
-                lse[...] = top + jnp.log(total)
+                lse[...] = top + jnp.log(total) * LOG2E
                 for h in range(heads):
                     part = slice(h * HEAD_DIM, (h + 1) * HEAD_DIM)
                     mixed[part, :] = (
@@ -183,7 +245,7 @@
 
         return carry
 
-    lax.fori_loop(0, tiles, attend_rest, 0)
+    lax.fori_loop(0, tiles, attend_rest, first)
 
     for s in range(stages):
         first = (frames - (frames >> s)) * per_block
@@ -216,16 +278,21 @@
     return pl.pallas_call(
         functools.partial(kernel, frames, groups, stages, tile, per_block, heads),
         out_shape=jax.ShapeDtypeStruct((own, width), bf16),
-        in_specs=[pl.BlockSpec(memory_space=pltpu.VMEM)] * 3,
+        in_specs=[pl.BlockSpec(memory_space=pl.ANY)] * 3,
         out_specs=pl.BlockSpec(memory_space=pltpu.VMEM),
         scratch_shapes=[
+            pltpu.VMEM((count, width), bf16),
+            pltpu.VMEM((rows, width), bf16),
+            pltpu.VMEM((rows, width), bf16),
+            pltpu.VMEM((2, max(rows, rest), tile), f32),
+            dma((3,)),
             pltpu.VMEM((groups - 1, rows, width), bf16),
             pltpu.VMEM((groups - 1, rows, width), bf16),
-            pltpu.VMEM((heads, rows, width), bf16),
+            pltpu.VMEM((heads, rows, 4 * HEAD_DIM), bf16),
             pltpu.VMEM((heads, wide, rows), bf16),
-            pltpu.VMEM((heads, rest, width), bf16),
+            pltpu.VMEM((heads, rest, 4 * HEAD_DIM), bf16),
             pltpu.VMEM((heads, wide, rest), bf16),
-            pltpu.VMEM((tiles, width, tile), bf16),
+            pltpu.VMEM((tiles, heads // 2, 4 * HEAD_DIM, tile), bf16),
             pltpu.VMEM((tiles, heads * wide, tile), f32),
             pltpu.VMEM((tiles, 8, tile), f32),
             pltpu.VMEM((width, tile), f32),
@@ -236,7 +303,7 @@
             dma((slots,)), dma((slots,)),
         ],
         compiler_params=pltpu.CompilerParams(
-            collective_id=0, has_side_effects=True, vmem_limit_bytes=48 * 1024 * 1024
+            collective_id=0, has_side_effects=True, vmem_limit_bytes=58 * 1024 * 1024
         ),
     )(queries, keys, values)
 

time: 75.8 us -> 56.1 us (0.74)
  Pallas kernels: 71.2 us -> 54.3 us
  local copies, waits for them, and re-layouts: 4.38 us -> 1.67 us
    pallas_call x1, Pallas kernels: 71.2 us -> 54.3 us  [local(): pl.pallas_call(functools.partial(kernel, frames, groups, stages, tile, pe...]
    unnamed x7 -> x1, local copies, waits for them, and re-layouts: 4.38 us -> 1.67 us
where the time goes in v2:
time: 56.1 us; the launch traced here: 55.9 us
  Pallas kernels  54.3 us (97%)
  local copies, waits for them, and re-layouts  1.67 us (3%)
    pallas_call x1, Pallas kernels, local(): pl.pallas_call(functools.partial(kernel, frames, groups, stages, tile, pe...  54.3 us
    unnamed x1, local copies, waits for them, and re-layouts  1.67 us

profile of v2, /device:TPU:0, one launch (start us, length us, event | category | flops | bytes accessed | tf_op | source)
XLA Modules:
  0.0 55.9 jit_solution(8479689535955227473)
XLA Ops:
  0.0 54.3 %shard_map.37 = bf16[512,256]{1,0:T(8,128)(2,1)} custom-call(bf16[4096,256]{1,0:T(8,128)(2,1)} %q_hbm.1, bf16[256,1024]{1,0:T(8,128)(2,1)} %k_ref.1, bf16[256,1024]{1,0:T(8,128)(2,1)} %v_ref.1), custom_call_target="tpu_custom_call" | custom-call | tf_op jit(solution)/shard_map/pallas_call | solution.py:278
  54.3 1.7 %copy.5 = bf16[512,256]{1,0:T(8,128)(2,1)} copy(bf16[512,256]{1,0:T(8,128)(2,1)} %shard_map.37) | data formatting | bytes 524288

commit v3 on v2

--- a/solution.py
+++ b/solution.py
@@ -28,8 +28,9 @@
         own = (column // HEAD_DIM) == h % 2
         kept = jnp.where(own, key_block[:, first : first + pair].astype(jnp.float32), 0.0)
         kept = kept.astype(jnp.bfloat16)
-        masked_ref[h, pl.ds(start, rows), 0:pair] = kept
-        masked_ref[h, pl.ds(start, rows), pair : 2 * pair] = kept
+        at = pl.ds((h % 2) * (masked_ref.shape[1] // 2) + start, rows)
+        masked_ref[h // 2, at, 0:pair] = kept
+        masked_ref[h // 2, at, pair : 2 * pair] = kept
         turned_ref[h, 0:HEAD_DIM, pl.ds(start, rows)] = turned[h * HEAD_DIM : (h + 1) * HEAD_DIM]
         turned_ref[h, HEAD_DIM : HEAD_DIM + ONES, pl.ds(start, rows)] = jnp.ones(
             (ONES, rows), jnp.bfloat16
@@ -107,40 +108,52 @@
             q_turned[t, g, pair : 2 * pair, :] = low[g * pair : (g + 1) * pair]
 
     def sweep(tile_of, masked, turned, floor, done):
-        depth = masked.shape[1]
+        depth = masked.shape[1] // 2
         step = min(256, depth)
-
-        def scores_of(t, h, slot, c):
-            at = slice(c * step, (c + 1) * step)
-            part = jnp.dot(masked[h, at, :], q_turned[t, h // 2], preferred_element_type=jnp.float32)
+        pairs = heads // 2
+        cuts = 1 if depth <= 256 else 2
+        rows = 2 * depth // cuts
+
+        def scores_of(t, g, slot, cut):
+            at = slice(cut * rows, (cut + 1) * rows)
+            part = jnp.dot(masked[g, at, :], q_turned[t, g], preferred_element_type=jnp.float32)
             score[slot, at, :] = part
-            return jnp.max(part, axis=0, keepdims=True)
-
-        first = floor(tile_of(0), 0)
-        for c in range(depth // step):
-            found = scores_of(tile_of(0), 0, 0, c)
-            first = found if first is None else jnp.maximum(first, found)
-
-        def visit(i, top):
+            return [
+                jnp.max(part[n * depth : (n + 1) * depth], axis=0, keepdims=True)
+                for n in range(2 // cuts)
+            ]
+
+        def lift(t, g, found):
+            low = [floor(t, 2 * g + n) for n in range(2)]
+            return tuple(f if b is None else jnp.maximum(f, b) for f, b in zip(found, low))
+
+        start = tile_of(0)
+        first = lift(start, 0, sum([scores_of(start, 0, 0, cut) for cut in range(cuts)], []))
+
+        def visit(i, tops):
             t = tile_of(i)
             after = tile_of(lax.rem(i + 1, tiles))
             if floor(t, 0) is None:
                 turn(after)
-            for h in range(heads):
-                slot = h % 2
-                where = (t, h + 1) if h + 1 < heads else (after, 0)
-                coming = floor(*where)
-                both = None
-                for c in range(depth // step):
-                    found = scores_of(*where, 1 - slot, c)
-                    coming = found if coming is None else jnp.maximum(coming, found)
-                    at = slice(c * step, (c + 1) * step)
-                    weights = jnp.exp2(score[slot, at, :] - top).astype(jnp.bfloat16)
-                    part = jnp.dot(turned[h, :, at], weights, preferred_element_type=jnp.float32)
-                    both = part if both is None else both + part
-                done(i, t, h, both, top)
-                top = coming
-            return top
+            for g in range(pairs):
+                slot = g % 2 if pairs % 2 == 0 else lax.rem(i * pairs + g, 2)
+                where = (t, g + 1) if g + 1 < pairs else (after, 0)
+                found = []
+                for n in range(2):
+                    if n < cuts:
+                        found += scores_of(*where, 1 - slot, n)
+                    both = None
+                    for c in range(depth // step):
+                        at = slice(n * depth + c * step, n * depth + (c + 1) * step)
+                        weights = jnp.exp2(score[slot, at, :] - tops[n]).astype(jnp.bfloat16)
+                        part = jnp.dot(
+                            turned[2 * g + n, :, c * step : (c + 1) * step], weights,
+                            preferred_element_type=jnp.float32,
+                        )
+                        both = part if both is None else both + part
+                    done(i, t, 2 * g + n, both, tops[n])
+                tops = lift(*where, found)
+            return tops
 
         return visit, first
 
@@ -278,19 +291,19 @@
     return pl.pallas_call(
         functools.partial(kernel, frames, groups, stages, tile, per_block, heads),
         out_shape=jax.ShapeDtypeStruct((own, width), bf16),
-        in_specs=[pl.BlockSpec(memory_space=pl.ANY)] * 3,
+        in_specs=[pl.BlockSpec(memory_space=pltpu.HBM)] * 3,
         out_specs=pl.BlockSpec(memory_space=pltpu.VMEM),
         scratch_shapes=[
             pltpu.VMEM((count, width), bf16),
             pltpu.VMEM((rows, width), bf16),
             pltpu.VMEM((rows, width), bf16),
-            pltpu.VMEM((2, max(rows, rest), tile), f32),
+            pltpu.VMEM((2, 2 * max(rows, rest), tile), f32),
             dma((3,)),
             pltpu.VMEM((groups - 1, rows, width), bf16),
             pltpu.VMEM((groups - 1, rows, width), bf16),
-            pltpu.VMEM((heads, rows, 4 * HEAD_DIM), bf16),
+            pltpu.VMEM((heads // 2, 2 * rows, 4 * HEAD_DIM), bf16),
             pltpu.VMEM((heads, wide, rows), bf16),
-            pltpu.VMEM((heads, rest, 4 * HEAD_DIM), bf16),
+            pltpu.VMEM((heads // 2, 2 * rest, 4 * HEAD_DIM), bf16),
             pltpu.VMEM((heads, wide, rest), bf16),
             pltpu.VMEM((tiles, heads // 2, 4 * HEAD_DIM, tile), bf16),
             pltpu.VMEM((tiles, heads * wide, tile), f32),
@@ -303,7 +316,7 @@
             dma((slots,)), dma((slots,)),
         ],
         compiler_params=pltpu.CompilerParams(
-            collective_id=0, has_side_effects=True, vmem_limit_bytes=58 * 1024 * 1024
+            collective_id=0, has_side_effects=True, vmem_limit_bytes=40 * 1024 * 1024
         ),
     )(queries, keys, values)
 

time: 56.1 us -> 55 us (0.980); the launches traced: 55.9 us -> 54 us
  Pallas kernels: 54.3 us -> 49.6 us
  local copies, waits for them, and re-layouts: 1.67 us -> 4.38 us
    pallas_call x1, Pallas kernels: 54.3 us -> 49.6 us  [local(): pl.pallas_call(functools.partial(kernel, frames, groups, stages, tile, pe...]
    unnamed x1 -> x7, local copies, waits for them, and re-layouts: 1.67 us -> 4.38 us
where the time goes in v3:
time: 55 us; the launch traced here: 54 us
  Pallas kernels  49.6 us (90%)
  local copies, waits for them, and re-layouts  4.38 us (8%)
    pallas_call x1, Pallas kernels, local(): pl.pallas_call(functools.partial(kernel, frames, groups, stages, tile, pe...  49.6 us
    unnamed x7, local copies, waits for them, and re-layouts  4.38 us

profile of v3, /device:TPU:0, one launch (start us, length us, event | category | flops | bytes accessed | tf_op | source)
XLA Modules:
  0.0 54.0 jit_solution(14065098802189906849)
XLA Ops:
  0.0 0.0 copy-start
  0.0 1.6 %copy-done = bf16[4096,256]{1,0:T(8,128)(2,1)S(1)} copy-done((bf16[4096,256]{1,0:T(8,128)(2,1)S(1)}, bf16[4096,256]{1,0:T(8,128)(2,1)}, u32[]{:S(2)}) %copy-start) | copy-done | bytes 2097176
  1.6 0.0 copy-start.1
  1.6 1.0 %copy-done.1 = bf16[256,1024]{1,0:T(8,128)(2,1)S(1)} copy-done((bf16[256,1024]{1,0:T(8,128)(2,1)S(1)}, bf16[256,1024]{1,0:T(8,128)(2,1)}, u32[]{:S(2)}) %copy-start.1) | copy-done | bytes 524312
  2.6 0.0 copy-start.2
  2.6 1.0 %copy-done.2 = bf16[256,1024]{1,0:T(8,128)(2,1)S(1)} copy-done((bf16[256,1024]{1,0:T(8,128)(2,1)S(1)}, bf16[256,1024]{1,0:T(8,128)(2,1)}, u32[]{:S(2)}) %copy-start.2) | copy-done | bytes 524312
  3.7 49.6 %shard_map.37 = bf16[512,256]{1,0:T(8,128)(2,1)S(1)} custom-call(bf16[4096,256]{1,0:T(8,128)(2,1)S(1)} %copy-done, bf16[256,1024]{1,0:T(8,128)(2,1)S(1)} %copy-done.1, bf16[256,1024]{1,0:T(8,128)(2,1)S(1)} %copy-done.2), custom_call_target="tpu_custom_call" | custom-call | tf_op jit(solution)/shard_map/pallas_call | solution.py:291
  53.3 0.7 %copy.5 = bf16[512,256]{1,0:T(8,128)(2,1)} copy(bf16[512,256]{1,0:T(8,128)(2,1)S(1)} %shard_map.37) | data formatting | bytes 524288
Async XLA Ops:
  0.0 1.6 %copy-start = (bf16[4096,256]{1,0:T(8,128)(2,1)S(1)}, bf16[4096,256]{1,0:T(8,128)(2,1)}, u32[]{:S(2)}) copy-start(bf16[4096,256]{1,0:T(8,128)(2,1)} %q_hbm.1) | copy-start | bytes 6291460
  1.6 1.0 %copy-start.1 = (bf16[256,1024]{1,0:T(8,128)(2,1)S(1)}, bf16[256,1024]{1,0:T(8,128)(2,1)}, u32[]{:S(2)}) copy-start(bf16[256,1024]{1,0:T(8,128)(2,1)} %k_ref.1) | copy-start | bytes 1572868
  2.6 1.0 %copy-start.2 = (bf16[256,1024]{1,0:T(8,128)(2,1)S(1)}, bf16[256,1024]{1,0:T(8,128)(2,1)}, u32[]{:S(2)}) copy-start(bf16[256,1024]{1,0:T(8,128)(2,1)} %v_ref.1) | copy-start | bytes 1572868

commit v4 on v3

--- a/solution.py
+++ b/solution.py
@@ -107,7 +107,7 @@
             q_turned[t, g, 0:pair, :] = high[g * pair : (g + 1) * pair]
             q_turned[t, g, pair : 2 * pair, :] = low[g * pair : (g + 1) * pair]
 
-    def sweep(tile_of, masked, turned, floor, done):
+    def sweep(tile_of, masked, turned, floor, done, opens=True):
         depth = masked.shape[1] // 2
         step = min(256, depth)
         pairs = heads // 2
@@ -127,8 +127,10 @@
             low = [floor(t, 2 * g + n) for n in range(2)]
             return tuple(f if b is None else jnp.maximum(f, b) for f, b in zip(found, low))
 
-        start = tile_of(0)
-        first = lift(start, 0, sum([scores_of(start, 0, 0, cut) for cut in range(cuts)], []))
+        first = None
+        if opens:
+            start = tile_of(0)
+            first = lift(start, 0, sum([scores_of(start, 0, 0, cut) for cut in range(cuts)], []))
 
         def visit(i, tops):
             t = tile_of(i)
@@ -163,7 +165,14 @@
 
     turn(0)
     visit_own, first = sweep(lambda i: i, masked_own, turned_own, lambda t, h: None, keep)
-    lax.fori_loop(0, tiles, visit_own, first)
+    together = 4 if tiles % 4 == 0 else 1
+
+    def attend_own(n, carry):
+        for u in range(together):
+            carry = visit_own(n * together + u, carry)
+        return carry
+
+    lax.fori_loop(0, tiles // together, attend_own, first)
 
     for d in range(1, groups):
         for copy in exchange(d):
@@ -196,69 +205,79 @@
             block = block + (1 << s) * ((bit(frame, s) + r) % 2)
         return rel, block * per_block + i % per_block
 
-    def settle(i, t, h, both, top):
+    def settle(j, i, t, h, both, top):
         before = early_top[t, h : h + 1, :]
         both = both + early[t, h * wide : (h + 1) * wide] * jnp.exp2(before - top)
         total = both[HEAD_DIM : HEAD_DIM + 1]
-        mixed[h * HEAD_DIM : (h + 1) * HEAD_DIM, :] = both[:HEAD_DIM] * (1.0 / total)
-        lse[h : h + 1, :] = top + jnp.log(total) * LOG2E
-
-    visit_rest, first = sweep(
-        lambda i: place(i)[1], masked_rest, turned_rest,
-        lambda t, h: early_top[t, h : h + 1, :], settle,
-    )
-
-    def attend_rest(i, carry):
-        j = i % per_block
-        rel, _ = place(i)
-        carry = visit_rest(i, carry)
+        mixed[j, h * HEAD_DIM : (h + 1) * HEAD_DIM, :] = both[:HEAD_DIM] * (1.0 / total)
+        lse[j, h : h + 1, :] = top + jnp.log(total) * LOG2E
+
+    rest_sweeps = [
+        sweep(
+            lambda i: place(i)[1], masked_rest, turned_rest,
+            lambda t, h: early_top[t, h : h + 1, :], functools.partial(settle, j), j == 0,
+        )
+        for j in range(per_block)
+    ]
+
+    def merge(s, rel, j):
+        slot = slot_of(s, rel, j)
+        part_copy(s, slot).wait_recv()
+        packed = inbox[slot, width:, :].astype(jnp.float32)
+        other = packed[0:8] + packed[8:16] + packed[16:24]
+        here = lse[j]
+        top = jnp.maximum(here, other)
+        a = jnp.exp2(here - top)
+        b = jnp.exp2(other - top)
+        total = a + b
+        a = a / total
+        b = b / total
+        lse[j] = top + jnp.log(total) * LOG2E
+        for h in range(heads):
+            part = slice(h * HEAD_DIM, (h + 1) * HEAD_DIM)
+            mixed[j, part, :] = (
+                mixed[j, part, :] * a[h : h + 1]
+                + inbox[slot, part, :].astype(jnp.float32) * b[h : h + 1]
+            )
+
+    def dispatch(s, rel, j):
+        slot = slot_of(s, rel, j)
+        outbox[slot, :width, :] = mixed[j].astype(jnp.bfloat16)
+        rest = lse[j]
+        pieces = []
+        for _ in range(3):
+            piece = rest.astype(jnp.bfloat16).astype(jnp.float32)
+            pieces.append(piece)
+            rest = rest - piece
+        pieces.append(jnp.zeros_like(rest))
+        outbox[slot, width:, :] = jnp.concatenate(pieces, axis=0).astype(jnp.bfloat16)
+        part_copy(s, slot).start()
+
+    def attend_rest(order, carry):
+        rel, _ = place(order * per_block)
+        for j in range(per_block):
+            carry = rest_sweeps[j][0](order * per_block + j, carry)
 
         for s in range(stages):
             @pl.when(rel % (1 << (s + 1)) == 0)
             def _():
-                slot = slot_of(s, rel, j)
-                part_copy(s, slot).wait_recv()
-                packed = inbox[slot, width:, :].astype(jnp.float32)
-                other = packed[0:8] + packed[8:16] + packed[16:24]
-                here = lse[...]
-                top = jnp.maximum(here, other)
-                a = jnp.exp2(here - top)
-                b = jnp.exp2(other - top)
-                total = a + b
-                a = a / total
-                b = b / total
-                lse[...] = top + jnp.log(total) * LOG2E
-                for h in range(heads):
-                    part = slice(h * HEAD_DIM, (h + 1) * HEAD_DIM)
-                    mixed[part, :] = (
-                        mixed[part, :] * a[h : h + 1]
-                        + inbox[slot, part, :].astype(jnp.float32) * b[h : h + 1]
-                    )
+                for j in range(per_block):
+                    merge(s, rel, j)
 
         for s in range(stages):
             @pl.when(rel % (1 << (s + 1)) == (1 << s))
             def _():
-                slot = slot_of(s, rel, j)
-                outbox[slot, :width, :] = mixed[...].astype(jnp.bfloat16)
-                rest = lse[...]
-                pieces = []
-                for _ in range(3):
-                    piece = rest.astype(jnp.bfloat16).astype(jnp.float32)
-                    pieces.append(piece)
-                    rest = rest - piece
-                pieces.append(jnp.zeros_like(rest))
-                outbox[slot, width:, :] = jnp.concatenate(pieces, axis=0).astype(jnp.bfloat16)
-                part_copy(s, slot).start()
+                for j in range(per_block):
+                    dispatch(s, rel, j)
 
         @pl.when(rel == 0)
         def _():
-            out_ref[pl.ds(pl.multiple_of(j * tile, tile), tile), :] = mixed[...].T.astype(
-                out_ref.dtype
-            )
+            for j in range(per_block):
+                out_ref[j * tile : (j + 1) * tile, :] = mixed[j].T.astype(out_ref.dtype)
 
         return carry
 
-    lax.fori_loop(0, tiles, attend_rest, first)
+    lax.fori_loop(0, frames, attend_rest, rest_sweeps[0][1])
 
     for s in range(stages):
         first = (frames - (frames >> s)) * per_block
@@ -291,7 +310,7 @@
     return pl.pallas_call(
         functools.partial(kernel, frames, groups, stages, tile, per_block, heads),
         out_shape=jax.ShapeDtypeStruct((own, width), bf16),
-        in_specs=[pl.BlockSpec(memory_space=pltpu.HBM)] * 3,
+        in_specs=[pl.BlockSpec(memory_space=pl.ANY)] * 3,
         out_specs=pl.BlockSpec(memory_space=pltpu.VMEM),
         scratch_shapes=[
             pltpu.VMEM((count, width), bf16),
@@ -308,15 +327,15 @@
             pltpu.VMEM((tiles, heads // 2, 4 * HEAD_DIM, tile), bf16),
             pltpu.VMEM((tiles, heads * wide, tile), f32),
             pltpu.VMEM((tiles, 8, tile), f32),
-            pltpu.VMEM((width, tile), f32),
-            pltpu.VMEM((8, tile), f32),
+            pltpu.VMEM((per_block, width, tile), f32),
+            pltpu.VMEM((per_block, 8, tile), f32),
             pltpu.VMEM((slots, width + LSE_ROWS, tile), bf16),
             pltpu.VMEM((slots, width + LSE_ROWS, tile), bf16),
             dma((groups - 1,)), dma((groups - 1,)), dma((groups - 1,)), dma((groups - 1,)),
             dma((slots,)), dma((slots,)),
         ],
         compiler_params=pltpu.CompilerParams(
-            collective_id=0, has_side_effects=True, vmem_limit_bytes=40 * 1024 * 1024
+            collective_id=0, has_side_effects=True, vmem_limit_bytes=58 * 1024 * 1024
         ),
     )(queries, keys, values)
 

time: 55 us -> 51.9 us (0.944)
  the two profiles are of different devices: /device:TPU:0 before, /device:TPU:1 now
where the time goes in v4:
time: 51.9 us; the launch traced here: 51.8 us
  Pallas kernels  50.1 us (97%)
  local copies, waits for them, and re-layouts  1.67 us (3%)
    pallas_call x1, Pallas kernels, local(): pl.pallas_call(functools.partial(kernel, frames, groups, stages, tile, pe...  50.1 us
    unnamed x1, local copies, waits for them, and re-layouts  1.67 us

profile of v4, /device:TPU:1, one launch (start us, length us, event | category | flops | bytes accessed | tf_op | source)
XLA Modules:
  0.0 51.8 jit_solution(11923902645684039298)
XLA Ops:
  0.0 50.1 %shard_map.37 = bf16[512,256]{1,0:T(8,128)(2,1)} custom-call(bf16[4096,256]{1,0:T(8,128)(2,1)} %q_hbm.1, bf16[256,1024]{1,0:T(8,128)(2,1)} %k_ref.1, bf16[256,1024]{1,0:T(8,128)(2,1)} %v_ref.1), custom_call_target="tpu_custom_call" | custom-call | tf_op jit(solution)/shard_map/pallas_call | solution.py:310
  50.1 1.7 %copy.5 = bf16[512,256]{1,0:T(8,128)(2,1)} copy(bf16[512,256]{1,0:T(8,128)(2,1)} %shard_map.37) | data formatting | bytes 524288

commit v5 on v4

--- a/solution.py
+++ b/solution.py
@@ -9,7 +9,7 @@
 
 HEAD_DIM = 64
 ONES = 16
-LSE_ROWS = 32
+LSE_ROWS = 16
 LOG2E = 1.4426950408889634
 MESH = pl.DeviceIdType.MESH
 
@@ -42,8 +42,9 @@
     q_hbm, k_ref, v_ref, out_ref,
     q_ref, k_own, v_own, score, local_sem,
     k_got, v_got, masked_own, turned_own, masked_rest, turned_rest,
-    q_turned, early, early_top, mixed, lse, outbox, inbox,
-    k_send, k_recv, v_send, v_recv, part_send, part_recv,
+    q_turned, early, early_top, mixed, lse, packing,
+    outbox_a, inbox_a, outbox_b, inbox_b,
+    k_send, k_recv, v_send, v_recv, send_a, recv_a, send_b, recv_b,
 ):
     frame = lax.axis_index("frame")
     group = lax.axis_index("head")
@@ -179,21 +180,31 @@
             copy.wait_recv()
         prepare(k_got[d - 1], v_got[d - 1], masked_rest, turned_rest, (d - 1) * rows, heads)
 
-    def part_copy(stage, slot):
+    swapped = (1, 0) + tuple(range(2, stages))
+    shares = (
+        (range(heads - 1), tuple(range(stages)), outbox_a, inbox_a, send_a, recv_a),
+        (range(heads - 1, heads), swapped, outbox_b, inbox_b, send_b, recv_b),
+    )
+
+    def part_copy(share, stage, slot):
+        _, bits, outbox, inbox, send, recv = share
         return pltpu.make_async_remote_copy(
             src_ref=outbox.at[slot],
             dst_ref=inbox.at[slot],
-            send_sem=part_send.at[slot],
-            recv_sem=part_recv.at[slot],
-            device_id=(partner(stage), group),
+            send_sem=send.at[slot],
+            recv_sem=recv.at[slot],
+            device_id=(partner(bits[stage]), group),
             device_id_type=MESH,
         )
+
+    def reorder(share, rel):
+        return sum((1 << s) * bit(rel, b) for s, b in enumerate(share[1]))
 
     def slot_of(stage, rel, j):
         first = frames - (frames >> stage)
         return (first + rel // (1 << (stage + 1))) * per_block + j
 
-    lse[...] = jnp.zeros_like(lse)
+    packing[...] = jnp.zeros_like(packing)
 
     def place(i):
         order = i // per_block
@@ -220,55 +231,68 @@
         for j in range(per_block)
     ]
 
-    def merge(s, rel, j):
+    def merge(share, s, rel, j):
+        mine_heads, inbox = share[0], share[3]
+        count = len(mine_heads)
         slot = slot_of(s, rel, j)
-        part_copy(s, slot).wait_recv()
-        packed = inbox[slot, width:, :].astype(jnp.float32)
-        other = packed[0:8] + packed[8:16] + packed[16:24]
-        here = lse[j]
-        top = jnp.maximum(here, other)
-        a = jnp.exp2(here - top)
-        b = jnp.exp2(other - top)
-        total = a + b
-        a = a / total
-        b = b / total
-        lse[j] = top + jnp.log(total) * LOG2E
-        for h in range(heads):
+        part_copy(share, s, slot).wait_recv()
+        packed = inbox[slot, count * HEAD_DIM :, :].astype(jnp.float32)
+        for n, h in enumerate(mine_heads):
+            other = sum(packed[count * p + n : count * p + n + 1] for p in range(3))
+            here = lse[j, h : h + 1, :]
+            top = jnp.maximum(here, other)
+            a = jnp.exp2(here - top)
+            b = jnp.exp2(other - top)
+            total = a + b
+            lse[j, h : h + 1, :] = top + jnp.log(total) * LOG2E
+            a = a / total
+            b = b / total
             part = slice(h * HEAD_DIM, (h + 1) * HEAD_DIM)
-            mixed[j, part, :] = (
-                mixed[j, part, :] * a[h : h + 1]
-                + inbox[slot, part, :].astype(jnp.float32) * b[h : h + 1]
-            )
-
-    def dispatch(s, rel, j):
+            there = inbox[slot, n * HEAD_DIM : (n + 1) * HEAD_DIM, :].astype(jnp.float32)
+            mixed[j, part, :] = mixed[j, part, :] * a + there * b
+
+    def dispatch(share, s, rel, j):
+        mine_heads, outbox = share[0], share[2]
+        count = len(mine_heads)
         slot = slot_of(s, rel, j)
-        outbox[slot, :width, :] = mixed[j].astype(jnp.bfloat16)
-        rest = lse[j]
-        pieces = []
-        for _ in range(3):
-            piece = rest.astype(jnp.bfloat16).astype(jnp.float32)
-            pieces.append(piece)
-            rest = rest - piece
-        pieces.append(jnp.zeros_like(rest))
-        outbox[slot, width:, :] = jnp.concatenate(pieces, axis=0).astype(jnp.bfloat16)
-        part_copy(s, slot).start()
+        first = mine_heads[0] * HEAD_DIM
+        outbox[slot, : count * HEAD_DIM, :] = mixed[j, first : first + count * HEAD_DIM, :].astype(
+            jnp.bfloat16
+        )
+        which = 0 if share is shares[0] else 1
+        for n, h in enumerate(mine_heads):
+            rest = lse[j, h : h + 1, :]
+            for p in range(3):
+                piece = rest.astype(jnp.bfloat16).astype(jnp.float32)
+                packing[which, j, count * p + n : count * p + n + 1, :] = piece
+                rest = rest - piece
+        outbox[slot, count * HEAD_DIM :, :] = packing[which, j].astype(jnp.bfloat16)
+        part_copy(share, s, slot).start()
 
     def attend_rest(order, carry):
         rel, _ = place(order * per_block)
         for j in range(per_block):
             carry = rest_sweeps[j][0](order * per_block + j, carry)
 
-        for s in range(stages):
-            @pl.when(rel % (1 << (s + 1)) == 0)
+        for share in shares:
+            @pl.when(reorder(share, rel) % 2 == 1)
             def _():
                 for j in range(per_block):
-                    merge(s, rel, j)
-
-        for s in range(stages):
-            @pl.when(rel % (1 << (s + 1)) == (1 << s))
-            def _():
-                for j in range(per_block):
-                    dispatch(s, rel, j)
+                    dispatch(share, 0, reorder(share, rel), j)
+
+        for share in shares:
+            turned_rel = reorder(share, rel)
+            for s in range(stages):
+                @pl.when(turned_rel % (1 << (s + 1)) == 0)
+                def _():
+                    for j in range(per_block):
+                        merge(share, s, turned_rel, j)
+
+            for s in range(1, stages):
+                @pl.when(turned_rel % (1 << (s + 1)) == (1 << s))
+                def _():
+                    for j in range(per_block):
+                        dispatch(share, s, turned_rel, j)
 
         @pl.when(rel == 0)
         def _():
@@ -279,15 +303,16 @@
 
     lax.fori_loop(0, frames, attend_rest, rest_sweeps[0][1])
 
-    for s in range(stages):
-        first = (frames - (frames >> s)) * per_block
-        count = (frames >> (s + 1)) * per_block
-
-        def drain(n, carry):
-            part_copy(s, first + n).wait_send()
-            return carry
-
-        lax.fori_loop(0, count, drain, 0)
+    for share in shares:
+        for s in range(stages):
+            first = (frames - (frames >> s)) * per_block
+            count = (frames >> (s + 1)) * per_block
+
+            def drain(n, carry):
+                part_copy(share, s, first + n).wait_send()
+                return carry
+
+            lax.fori_loop(0, count, drain, 0)
     for d in range(1, groups):
         for copy in exchange(d):
             copy.wait_send()
@@ -305,6 +330,7 @@
     slots = (frames - 1) * per_block
     rest = (groups - 1) * rows
     wide = HEAD_DIM + ONES
+    main = width - HEAD_DIM + LSE_ROWS
     bf16, f32 = jnp.bfloat16, jnp.float32
     dma = pltpu.SemaphoreType.DMA
     return pl.pallas_call(
@@ -329,13 +355,16 @@
             pltpu.VMEM((tiles, 8, tile), f32),
             pltpu.VMEM((per_block, width, tile), f32),
             pltpu.VMEM((per_block, 8, tile), f32),
-            pltpu.VMEM((slots, width + LSE_ROWS, tile), bf16),
-            pltpu.VMEM((slots, width + LSE_ROWS, tile), bf16),
+            pltpu.VMEM((2, per_block, LSE_ROWS, tile), f32),
+            pltpu.VMEM((slots, main, tile), bf16),
+            pltpu.VMEM((slots, main, tile), bf16),
+            pltpu.VMEM((slots, HEAD_DIM + LSE_ROWS, tile), bf16),
+            pltpu.VMEM((slots, HEAD_DIM + LSE_ROWS, tile), bf16),
             dma((groups - 1,)), dma((groups - 1,)), dma((groups - 1,)), dma((groups - 1,)),
-            dma((slots,)), dma((slots,)),
+            dma((slots,)), dma((slots,)), dma((slots,)), dma((slots,)),
         ],
         compiler_params=pltpu.CompilerParams(
-            collective_id=0, has_side_effects=True, vmem_limit_bytes=58 * 1024 * 1024
+            collective_id=0, has_side_effects=True, vmem_limit_bytes=56_000_000
         ),
     )(queries, keys, values)
 

time: 51.9 us -> 47.5 us (0.915)
  Pallas kernels: 50.1 us -> 46.7 us
  local copies, waits for them, and re-layouts: 1.67 us -> 0.71 us
    pallas_call x1, Pallas kernels: 50.1 us -> 46.7 us  [local(): pl.pallas_call(functools.partial(kernel, frames, groups, stages, tile, pe...]
    unnamed x1, local copies, waits for them, and re-layouts: 1.67 us -> 0.71 us
where the time goes in v5:
time: 47.5 us; the launch traced here: 47.4 us
  Pallas kernels  46.7 us (98%)
  local copies, waits for them, and re-layouts  0.71 us (1%)
    pallas_call x1, Pallas kernels, local(): pl.pallas_call(functools.partial(kernel, frames, groups, stages, tile, pe...  46.7 us

profile of v5, /device:TPU:1, one launch (start us, length us, event | category | flops | bytes accessed | tf_op | source)
XLA Modules:
  0.0 47.4 jit_solution(8735681100649657396)
XLA Ops:
  0.0 46.7 %shard_map.37 = bf16[512,256]{1,0:T(8,128)(2,1)S(1)} custom-call(bf16[4096,256]{1,0:T(8,128)(2,1)} %q_hbm.1, bf16[256,1024]{1,0:T(8,128)(2,1)} %k_ref.1, bf16[256,1024]{1,0:T(8,128)(2,1)} %v_ref.1), custom_call_target="tpu_custom_call" | custom-call | tf_op jit(solution)/shard_map/pallas_call | solution.py:336
  46.7 0.7 %copy.5 = bf16[512,256]{1,0:T(8,128)(2,1)} copy(bf16[512,256]{1,0:T(8,128)(2,1)S(1)} %shard_map.37) | data formatting | bytes 524288

commit v6 on v5

--- a/solution.py
+++ b/solution.py
@@ -53,6 +53,11 @@
     wide = HEAD_DIM + ONES
     tiles = frames * per_block
 
+    def member(d):
+        return sum(
+            (1 << p) * ((bit(group, p) + bit(d, p)) % 2) for p in range(groups.bit_length() - 1)
+        )
+
     def partner(stage):
         return frame + (1 << stage) * (1 - 2 * bit(frame, stage))
 
@@ -68,14 +73,14 @@
     barrier = pltpu.get_barrier_semaphore()
     for d in range(1, groups):
         pl.semaphore_signal(
-            barrier, inc=1, device_id=(frame, lax.rem(group + d, groups)), device_id_type=MESH
+            barrier, inc=1, device_id=(frame, member(d)), device_id_type=MESH
         )
     for s in range(stages):
         pl.semaphore_signal(barrier, inc=1, device_id=(partner(s), group), device_id_type=MESH)
     pl.semaphore_wait(barrier, groups - 1 + stages)
 
     def exchange(d):
-        to = lax.rem(group + d, groups)
+        to = member(d)
         columns = pl.ds(pl.multiple_of(to * width, width), width)
         return [
             pltpu.make_async_remote_copy(
@@ -89,7 +94,7 @@
             for ref, got, send, recv in ((k_ref, k_got, k_send, k_recv), (v_ref, v_got, v_send, v_recv))
         ]
 
-    for d in range(1, groups):
+    for d in [*range(2, groups), 1]:
         for copy in exchange(d):
             copy.start()
 

time: 47.5 us -> 52.6 us (1.11)
  the two profiles are of different devices: /device:TPU:1 before, /device:TPU:0 now
where the time goes in v6:
time: 52.6 us; the launch traced here: 52.4 us
  Pallas kernels  51.7 us (98%)
  local copies, waits for them, and re-layouts  0.71 us (1%)
    pallas_call x1, Pallas kernels, local(): pl.pallas_call(functools.partial(kernel, frames, groups, stages, tile, pe...  51.7 us

profile of v6, /device:TPU:0, one launch (start us, length us, event | category | flops | bytes accessed | tf_op | source)
XLA Modules:
  0.0 52.4 jit_solution(3068991632860148849)
XLA Ops:
  0.0 51.7 %shard_map.37 = bf16[512,256]{1,0:T(8,128)(2,1)S(1)} custom-call(bf16[4096,256]{1,0:T(8,128)(2,1)} %q_hbm.1, bf16[256,1024]{1,0:T(8,128)(2,1)} %k_ref.1, bf16[256,1024]{1,0:T(8,128)(2,1)} %v_ref.1), custom_call_target="tpu_custom_call" | custom-call | tf_op jit(solution)/shard_map/pallas_call | solution.py:341
  51.7 0.7 %copy.5 = bf16[512,256]{1,0:T(8,128)(2,1)} copy(bf16[512,256]{1,0:T(8,128)(2,1)S(1)} %shard_map.37) | data formatting | bytes 524288

commit v7 on v6

--- a/solution.py
+++ b/solution.py
@@ -94,7 +94,7 @@
             for ref, got, send, recv in ((k_ref, k_got, k_send, k_recv), (v_ref, v_got, v_send, v_recv))
         ]
 
-    for d in [*range(2, groups), 1]:
+    for d in range(1, groups):
         for copy in exchange(d):
             copy.start()
 
@@ -102,6 +102,9 @@
     fetches[1].wait()
     prepare(k_own[...], v_own[...], masked_own, turned_own, 0, heads)
     fetches[2].wait()
+    for copy in exchange(1):
+        copy.wait_recv()
+    prepare(k_got[0], v_got[0], masked_own, turned_own, rows, heads)
 
     def turn(t):
         q = q_ref[pl.ds(pl.multiple_of(t * tile, tile), tile), :].astype(jnp.float32).T
@@ -171,7 +174,7 @@
 
     turn(0)
     visit_own, first = sweep(lambda i: i, masked_own, turned_own, lambda t, h: None, keep)
-    together = 4 if tiles % 4 == 0 else 1
+    together = 2 if tiles % 2 == 0 else 1
 
     def attend_own(n, carry):
         for u in range(together):
@@ -180,10 +183,10 @@
 
     lax.fori_loop(0, tiles // together, attend_own, first)
 
-    for d in range(1, groups):
+    for d in range(2, groups):
         for copy in exchange(d):
             copy.wait_recv()
-        prepare(k_got[d - 1], v_got[d - 1], masked_rest, turned_rest, (d - 1) * rows, heads)
+        prepare(k_got[d - 1], v_got[d - 1], masked_rest, turned_rest, (d - 2) * rows, heads)
 
     swapped = (1, 0) + tuple(range(2, stages))
     shares = (
@@ -333,7 +336,7 @@
     per_block = own // tile
     tiles = count // tile
     slots = (frames - 1) * per_block
-    rest = (groups - 1) * rows
+    rest = (groups - 2) * rows
     wide = HEAD_DIM + ONES
     main = width - HEAD_DIM + LSE_ROWS
     bf16, f32 = jnp.bfloat16, jnp.float32
@@ -347,12 +350,12 @@
             pltpu.VMEM((count, width), bf16),
             pltpu.VMEM((rows, width), bf16),
             pltpu.VMEM((rows, width), bf16),
-            pltpu.VMEM((2, 2 * max(rows, rest), tile), f32),
+            pltpu.VMEM((2, 2 * max(2 * rows, rest), tile), f32),
             dma((3,)),
             pltpu.VMEM((groups - 1, rows, width), bf16),
             pltpu.VMEM((groups - 1, rows, width), bf16),
-            pltpu.VMEM((heads // 2, 2 * rows, 4 * HEAD_DIM), bf16),
-            pltpu.VMEM((heads, wide, rows), bf16),
+            pltpu.VMEM((heads // 2, 4 * rows, 4 * HEAD_DIM), bf16),
+            pltpu.VMEM((heads, wide, 2 * rows), bf16),
             pltpu.VMEM((heads // 2, 2 * rest, 4 * HEAD_DIM), bf16),
             pltpu.VMEM((heads, wide, rest), bf16),
             pltpu.VMEM((tiles, heads // 2, 4 * HEAD_DIM, tile), bf16),

time: 52.6 us -> 52.1 us (level)
  no operation moved by 1% of the time
where the time goes in v7:
time: 52.1 us; the launch traced here: 52 us
  Pallas kernels  51.2 us (98%)
  local copies, waits for them, and re-layouts  0.71 us (1%)
    pallas_call x1, Pallas kernels, local(): pl.pallas_call(functools.partial(kernel, frames, groups, stages, tile, pe...  51.2 us

profile of v7, /device:TPU:0, one launch (start us, length us, event | category | flops | bytes accessed | tf_op | source)
XLA Modules:
  0.0 52.0 jit_solution(16560566447147186504)
XLA Ops:
  0.0 51.2 %shard_map.37 = bf16[512,256]{1,0:T(8,128)(2,1)S(1)} custom-call(bf16[4096,256]{1,0:T(8,128)(2,1)} %q_hbm.1, bf16[256,1024]{1,0:T(8,128)(2,1)} %k_ref.1, bf16[256,1024]{1,0:T(8,128)(2,1)} %v_ref.1), custom_call_target="tpu_custom_call" | custom-call | tf_op jit(solution)/shard_map/pallas_call | solution.py:344
  51.3 0.7 %copy.5 = bf16[512,256]{1,0:T(8,128)(2,1)} copy(bf16[512,256]{1,0:T(8,128)(2,1)S(1)} %shard_map.37) | data formatting | bytes 524288
